TPU v7x, 128 devices: a whole 4x4x4 slice. The times are simulated.
128 devices in a mesh: rows: 4 (over z_lo, core), cols: 32 (over y, x, z_hi).
Axes of the slice: x: 4, y: 4, z: 4 (z_hi: 2, z_lo: 2; z = z_hi * 2 + z_lo), core: 2. Of those that a mesh axis runs over, the one named last changes fastest.
Arguments:
- pair_integrals: float32 [4096, 16384], P('rows', 'cols'), may hold values from -6 to 6
- left_factor: float32 [4096, 1024], P('rows', 'cols'), may hold values from -0.9375 to 0.9375
- core: float32 [1024, 1024], replicated, may hold values from -6 to 6
- right_factor: float32 [16384, 1024], P('cols', 'rows'), may hold values from -0.46875 to 0.46875
Outputs:
- core_next: float32 [1024, 1024], replicated
All inputs are finite; a program needn't handle non-finite values.
Results may differ from a plain program's by a relative error of at most 0.000062.
Values sent between devices are 32-bit elements; how exact they have to be, the bound alone decides.
A program may use at most 128 MiB of HBM per device.

v0:
```python
import functools

import jax
import jax.numpy as jnp
from jax import lax
from jax.sharding import Mesh
from jax.sharding import PartitionSpec as P

COLS = ("cols_0", "cols_1", "cols_2")
ROWS = ("rows_0", "rows_1")
ROWS_COLS = ("rows_0", "rows_1", "cols_0", "cols_1", "cols_2")


def joined_along(parts, dim):
    shape = list(parts.shape[1:])
    shape[dim] *= parts.shape[0]
    return jnp.moveaxis(parts, 0, dim).reshape(shape)


def copy_for_each(x, axis):
    devices = lax.axis_size(axis)
    return lax.all_to_all(jnp.broadcast_to(x[None], (devices, *x.shape)), axis, 0, 0, tiled=True)


def gathered_copies(x, axis, dim):
    return joined_along(copy_for_each(x, axis), dim)


def one_axis_at_a_time(x, axes):
    return functools.reduce(lax.psum, axes, x)


def product(left, right):
    return jnp.dot(left, right, precision=lax.Precision.HIGHEST, preferred_element_type=jnp.float32)


def shards(pair_integrals, left_factor, core, right_factor):
    left_rows = lax.all_gather(left_factor, COLS, axis=1, tiled=True)
    right_rows = gathered_copies(right_factor, ROWS, 1)
    mixed = product(core, right_rows.T)
    residual = pair_integrals - product(left_rows, mixed)
    along = product(residual, right_rows)
    local_term = product(left_rows.T, along)
    gradient = lax.psum(local_term, ROWS_COLS)
    numer = jnp.sum(gradient * gradient)
    image = product(left_rows, product(gradient, right_rows.T))
    denom = one_axis_at_a_time(jnp.sum(image * image), ROWS_COLS)
    return core + numer / denom * gradient


def solution(mesh):
    finer = Mesh(
        mesh.devices.reshape(2, 2, 4, 4, 2), ("rows_0", "rows_1", "cols_0", "cols_1", "cols_2")
    )
    placed = (P(ROWS, COLS), P(ROWS, COLS), P(), P(COLS, ROWS))
    return jax.shard_map(shards, mesh=finer, in_specs=placed, out_specs=P(), check_vma=False)
```

profile of v0, /device:TPU:0, one launch (start us, length us, event | category | flops | bytes accessed | tf_op | source)
XLA Modules:
  0.0 376.6 jit_solution(10287196216406322099)
XLA Ops:
  6.5 0.0 all-gather.2.cloned.1.call-start
  6.5 0.7 all-gather.2.cloned.1.call-update
  7.3 0.0 all-reduce.2.cloned.1.call-start
  7.3 1.2 copy.7
  8.5 0.0 copy-start
  8.6 0.3 broadcast_in_dim.2
  8.8 30.0 %all_to_all.5 = f32[4,512,256]{1,2,0:T(8,128)S(1)} all-to-all(f32[4,512,256]{1,2,0:T(8,128)S(1)} %broadcast_in_dim.2), channel_id=1, replica_groups=mesh['rows_0'=2,'rows_1'=2,'cols_0'=4,'cols_1'=4,'cols_2'=2] {'rows_0','..., dimensions={0} | all-to-all | bytes 4194304 | tf_op jit(solution)/shard_map/all_to_all | solution.py:22
  38.8 0.0 copy-done
  38.8 8.0 %fusion.1 = f32[1024,512]{1,0:T(8,128)} fusion(f32[1024,1024]{1,0:T(8,128)S(1)} %copy-done, f32[512,1024]{0,1:T(8,128)S(1)} %bitcast.19), kind=kOutput, calls=%fused_computation.6 | convolution fusion | flops 6442450944 | bytes 8388608 | tf_op jit(solution)/shard_map/dot_general | solution.py:34
  46.8 48.8 %all-gather.2.cloned.1.call-done = f32[1024,1024]{0,1:T(8,128)} async-done(((f32[1024,32]{0,1:T(8,128)}), f32[1024,1024]{0,1:T(8,128)}) %all-gather.2.cloned.1.call-update) | async-done | bytes 4194320 | tf_op jit(solution)/shard_map/all_gather | solution.py:38
  95.6 0.0 copy-start.3
  95.6 9.9 %fusion.2 = f32[512,1024]{0,1:T(8,128)S(1)} fusion(f32[1024,512]{1,0:T(8,128)} %fusion.1, f32[1024,1024]{0,1:T(8,128)} %all-gather.2.cloned.1.call-done), kind=kOutput, calls=%fused_computation.7 | convolution fusion | flops 6442450944 | bytes 8388608 | tf_op jit(solution)/shard_map/dot_general | solution.py:34
  105.6 0.0 copy-done.3
  105.6 0.0 copy-start.1
  105.6 6.9 %fusion = f32[1024,1024]{1,0:T(8,128)S(1)} fusion(f32[512,1024]{0,1:T(8,128)S(1)} %bitcast.20, f32[1024,512]{1,0:T(8,128)S(1)} %copy-done.3, f32[512,1024]{0,1:T(8,128)S(1)} %fusion.2), kind=kOutput, calls=%fused_computation.4 | convolution fusion | flops 6442975232 | bytes 10485760 | tf_op jit(solution)/shard_map/dot_general | solution.py:34
  112.5 0.0 copy-done.1
  112.5 29.8 %convolution_bitcast_fusion = f32[1024,1024]{0,1:T(8,128)} fusion(f32[1024,1024]{1,0:T(8,128)S(1)} %fusion, f32[1024,1024]{0,1:T(8,128)S(1)} %copy-done.1), kind=kOutput, calls=%fused_computation.2 | convolution fusion | flops 12884901888 | bytes 12582912 | tf_op jit(solution)/shard_map/dot_general | solution.py:34
  142.3 0.0 all-reduce.2.cloned.1.call-update
  142.3 150.9 %all-reduce.2.cloned.1.call-done = f32[1024,1024]{0,1:T(8,128)} async-done(((f32[1024,1024]{0,1:T(8,128)}), f32[1024,1024]{0,1:T(8,128)}) %all-reduce.2.cloned.1.call-update) | async-done | bytes 4194320 | tf_op jit(solution)/shard_map/psum | solution.py:44
  293.2 0.0 copy-start.2
  293.2 8.8 %fusion.3 = f32[1024,512]{1,0:T(8,128)S(1)} fusion(f32[1024,1024]{0,1:T(8,128)} %all-reduce.2.cloned.1.call-done, f32[512,1024]{0,1:T(8,128)S(1)} %bitcast.21), kind=kOutput, calls=%fused_computation.8 | convolution fusion | flops 6442450944 | bytes 8388608 | tf_op jit(solution)/shard_map/dot_general | solution.py:34
  302.0 0.0 copy-done.2
  302.0 7.8 %multiply_reduce_fusion.1 = f32[]{:T(128)} fusion(f32[1024,512]{1,0:T(8,128)S(1)} %fusion.3, f32[1024,1024]{0,1:T(8,128)S(1)} %copy-done.2), kind=kOutput, calls=%fused_computation.5 | convolution fusion | flops 6443499520 | bytes 6291460 | tf_op jit(solution)/shard_map/dot_general | solution.py:34
  309.8 5.5 %psum.43 = f32[]{:T(128)} all-reduce(f32[]{:T(128)} %multiply_reduce_fusion.1), channel_id=1, replica_groups=mesh['rows_0'=2,'rows_1'=2,'cols_0'=4,'cols_1'=4,'cols_2'=2] {'rows_0'}, use_global_device_ids=true, to_apply=%region_3.0 | all-reduce | flops 1 | bytes 8 | tf_op jit(solution)/shard_map/psum | solution.py:30
  315.4 3.1 psum.44
  318.4 10.2 %psum.45 = f32[]{:T(128)} all-reduce(f32[]{:T(128)} %psum.44), channel_id=1, replica_groups=mesh['rows_0'=2,'rows_1'=2,'cols_0'=4,'cols_1'=4,'cols_2'=2] {'cols_0'}, use_global_device_ids=true, to_apply=%region_5.0 | all-reduce | flops 1 | bytes 8 | tf_op jit(solution)/shard_map/psum | solution.py:30
  328.7 11.1 %psum.46 = f32[]{:T(128)} all-reduce(f32[]{:T(128)} %psum.45), channel_id=1, replica_groups=mesh['rows_0'=2,'rows_1'=2,'cols_0'=4,'cols_1'=4,'cols_2'=2] {'cols_1'}, use_global_device_ids=true, to_apply=%region_6.0 | all-reduce | flops 1 | bytes 8 | tf_op jit(solution)/shard_map/psum | solution.py:30
  339.8 5.3 %copy.8 = f32[1024,1024]{0,1:T(8,128)} copy(f32[1024,1024]{1,0:T(8,128)} %param.6) | data formatting | bytes 8388608 | tf_op args[2]
  345.1 7.1 %psum.47 = f32[]{:T(128)} all-reduce(f32[]{:T(128)} %psum.46), channel_id=1, replica_groups=mesh['rows_0'=2,'rows_1'=2,'cols_0'=4,'cols_1'=4,'cols_2'=2] {'cols_2'}, use_global_device_ids=true, to_apply=%region_7.0 | all-reduce | flops 1 | bytes 8 | tf_op jit(solution)/shard_map/psum | solution.py:30
  352.2 3.9 %multiply_reduce_fusion = f32[]{:T(128)} fusion(f32[1024,1024]{0,1:T(8,128)} %all-reduce.2.cloned.1.call-done), kind=kLoop, calls=%fused_computation.1 | loop fusion | flops 2097151 | bytes 4194308 | tf_op jit(solution)/shard_map/reduce_sum | solution.py:45
  357.3 6.9 %multiply_add_fusion = f32[1024,1024]{0,1:T(8,128)} fusion(f32[1024,1024]{0,1:T(8,128)} %copy.8, f32[1024,1024]{0,1:T(8,128)} %all-reduce.2.cloned.1.call-done, f32[]{:T(128)S(6)} %div.3), kind=kLoop, calls=%fused_computation | loop fusion | flops 2097152 | bytes 12582916 | tf_op jit(solution)/shard_map/add | solution.py:48
  364.2 5.3 %copy.9 = f32[1024,1024]{1,0:T(8,128)} copy(f32[1024,1024]{0,1:T(8,128)} %multiply_add_fusion) | data formatting | bytes 8388608 | tf_op jit(solution)/shard_map/add | solution.py:48
Async XLA Ops:
  6.5 89.1 %all-gather.2.cloned.1.call-start = ((), (), s32[]{:S(2)}) async-start(), calls=%async_computation.1 | async-start | bytes 4325376 | tf_op jit(solution)/shard_map/all_gather | solution.py:38
  7.3 286.0 %all-reduce.2.cloned.1.call-start = ((), (), s32[]{:S(2)}) async-start(), calls=%async_computation.2 | async-start | bytes 8388608 | tf_op jit(solution)/shard_map/psum | solution.py:44
  8.5 30.2 %copy-start = (f32[1024,1024]{1,0:T(8,128)S(1)}, f32[1024,1024]{1,0:T(8,128)}, u32[]{:S(2)}) copy-start(f32[1024,1024]{1,0:T(8,128)} %param.6) | copy-start | bytes 12582916
  95.6 9.9 %copy-start.3 = (f32[1024,512]{1,0:T(8,128)S(1)}, f32[1024,512]{1,0:T(8,128)}, u32[]{:S(2)}) copy-start(f32[1024,512]{1,0:T(8,128)} %param.4) | copy-start | bytes 6291460
  105.6 6.9 %copy-start.1 = (f32[1024,1024]{0,1:T(8,128)S(1)}, f32[1024,1024]{0,1:T(8,128)}, u32[]{:S(2)}) copy-start(f32[1024,1024]{0,1:T(8,128)} %all-gather.2.cloned.1.call-done) | copy-start | bytes 12582916
  293.2 8.8 %copy-start.2 = (f32[1024,1024]{0,1:T(8,128)S(1)}, f32[1024,1024]{0,1:T(8,128)}, u32[]{:S(2)}) copy-start(f32[1024,1024]{0,1:T(8,128)} %all-gather.2.cloned.1.call-done) | copy-start | bytes 12582916
Sparse Core Ops, SparseCore 0:
  10.3 85.2 all-gather.1
  142.4 150.7 all-reduce.1
where the time goes:
time: 384 us; the launch traced here: 377 us
  waiting for transfers between devices  201 us (52%)
  matrix products  71.1 us (19%)
  blocking collectives  67 us (17%)
  between operations  15 us (4%)
  local copies, waits for them, and re-layouts  12.2 us (3%)
  other arithmetic  10.7 us (3%)
    psum x1, waiting for transfers between devices, shards(): gradient = lax.psum(local_term, ROWS_COLS)  151 us
    dot_general x6, matrix products, product(): jnp.dot(left, right, precision=lax.Precision.HIGHEST, preferred_element_t...  71.1 us
    all_gather x1, waiting for transfers between devices, shards(): left_rows = lax.all_gather(left_factor, COLS, axis=1, tiled=True)  48.8 us
    psum x5, blocking collectives, one_axis_at_a_time(): return functools.reduce(lax.psum, axes, x)  37.1 us
    all_to_all x1, blocking collectives, copy_for_each(): lax.all_to_all(jnp.broadcast_to(x[None], (devices, *x.shape)), axis, 0, 0...  30 us
  transfers between devices with their start and end apart: 2, of which 2 were waited for; matrix products, arithmetic and copies ran while one was open for 3% of the time, Pallas kernels for 0%

commit v1 on v0

v1 whole, which is shorter than its diff:
```python
import functools

import jax
import jax.numpy as jnp
from jax import lax
from jax.experimental import pallas as pl
from jax.experimental.pallas import tpu as pltpu
from jax.sharding import PartitionSpec as P

MESH = pl.DeviceIdType.MESH
F32, BF16 = jnp.float32, jnp.bfloat16
GROUPS = ((0, 384, "xyz"), (384, 384, "yzx"), (768, 256, "zxy"))
MESSAGES = 160
NN = (((1,), (0,)), ((), ()))
NT = (((1,), (1,)), ((), ()))


def split(v):
    hi = v.astype(BF16)
    return hi, (v - hi.astype(F32)).astype(BF16)


def dot3(ah, al, bh, bl, dims):
    dot = functools.partial(lax.dot_general, dimension_numbers=dims, preferred_element_type=F32)
    return dot(ah, bh) + dot(ah, bl) + dot(al, bh)


def aligned(i, m):
    return pl.multiple_of(i, m)


class Sender:
    def __init__(self, send_sems, recv_sems):
        self.send_sems, self.recv_sems, self.sent = send_sems, recv_sems, []

    def __call__(self, src, dst, peer):
        i = len(self.sent)
        copy = pltpu.make_async_remote_copy(
            src_ref=src,
            dst_ref=dst,
            send_sem=self.send_sems.at[i],
            recv_sem=self.recv_sems.at[i],
            device_id=peer,
            device_id_type=MESH,
        )
        copy.start()
        self.sent.append(copy)
        return copy


def lockstep(generators):
    live = list(generators)
    while live:
        still = []
        for g in live:
            try:
                next(g)
                still.append(g)
            except StopIteration:
                pass
        live = still


def kernel(
    v_hbm, l_hbm, z_hbm, r_hbm, g_hbm, step_ref,
    l_in, v_in, z_in, lt, r4, rest, u, u_in, g,
    zh, zl, rh, rl, lth, ltl, mh, ml, resh, resl, uh, ul, gch, gcl, ih, il,
    gp_a, gp_b, gp_c, relay_a, relay_b, relay_c, ra_a, ra_b, ra_c,
    acc_a, acc_b, acc_c, rb_a, rb_b, rb_c, accb_a, accb_b, accb_c, rc_a, rc_b, rc_c,
    slots, send_sems, recv_sems, local_sems,
):
    r, c = lax.axis_index("rows"), lax.axis_index("cols")
    core, z_lo, z_hi = lax.rem(r, 2), lax.div(r, 2), lax.rem(c, 2)
    x, y, z = lax.rem(lax.div(c, 2), 4), lax.div(c, 8), 2 * z_hi + z_lo
    other = 1 - core

    def device(dx, dy, dz, k):
        xx, yy, zz = lax.rem(x + dx, 4), lax.rem(y + dy, 4), lax.rem(z + dz, 4)
        return (2 * lax.rem(zz, 2) + k, 8 * yy + 2 * xx + lax.div(zz, 2))

    peer = {
        "x": [device(d, 0, 0, core) for d in range(4)],
        "y": [device(0, d, 0, core) for d in range(4)],
        "z": [device(0, 0, d, core) for d in range(4)],
    }
    coord = {"x": x, "y": y, "z": z}
    partner = device(0, 0, 0, other)
    z_lo_partner = (2 * (1 - z_lo) + core, c)
    z_hi_partner = peer["z"][2]
    first = [device(d * other, d * core, 0, core) for d in range(4)]
    second = [device(d * core, d * other, 0, core) for d in range(4)]
    i1, i2 = x * other + y * core, y * other + x * core

    copy_l = pltpu.make_async_copy(l_hbm, l_in, local_sems.at[0])
    copy_r = pltpu.make_async_copy(r_hbm, r4.at[r], local_sems.at[1])
    copy_v = pltpu.make_async_copy(v_hbm, v_in, local_sems.at[2])
    copy_l.start()
    copy_r.start()
    copy_v.start()
    copy_z = []
    for b in range(16):
        by, bx = b // 4, b % 4
        at2, at1 = by * other + bx * core, bx * other + by * core
        copy_z.append(
            pltpu.make_async_copy(
                z_hbm.at[pl.ds(64 * b, 64), :],
                z_in.at[at2, pl.ds(aligned(64 * at1, 64), 64), :],
                local_sems.at[4 + b],
            )
        )
        copy_z[-1].start()

    barrier = pltpu.get_barrier_semaphore()
    greeted = [partner] + [peer[a][d] for a in "xyz" for d in (1, 2, 3)]
    for other_device in greeted:
        pl.semaphore_signal(barrier, inc=1, device_id=other_device, device_id_type=MESH)
    pl.semaphore_wait(barrier, len(greeted))

    send = Sender(send_sems, recv_sems)

    def shard(d1, d2, h):
        at1, at2 = lax.rem(i1 + d1, 4), lax.rem(i2 + d2, 4)
        return lt.at[at2, pl.ds(aligned(64 * at1 + 32 * h, 32), 32), :]

    def spread(ref, peers):
        return send(ref, ref, peers[1]), send(ref, ref, peers[3])

    own, far = z_hi, 1 - z_hi
    copy_l.wait()
    lt[i2, pl.ds(aligned(64 * i1 + 32 * own, 32), 32), :] = jnp.transpose(l_in[...])
    mine = shard(0, 0, own)
    to_z = send(mine, mine, z_hi_partner)
    near_own = spread(mine, first)
    wide = {(0, "own"): spread(mine, second)}

    copy_r.wait()
    r_to_core = send(r4.at[r], r4.at[r], partner)
    r_to_z = send(r4.at[r], r4.at[r], z_lo_partner)

    def transpose_v(i):
        rest[:, 128 * i : 128 * i + 128] = jnp.transpose(v_in[128 * i : 128 * i + 128, :])

    copy_v.wait()
    for i in range(4):
        transpose_v(i)

    to_z.wait_recv()
    theirs = shard(0, 0, far)
    near_far = spread(theirs, first)
    wide[0, "far"] = spread(theirs, second)
    for i in range(4, 8):
        transpose_v(i)

    near_own[0].wait_recv()
    ref = shard(3, 0, own)
    through_own = send(ref, ref, first[1])
    wide[3, "own"] = spread(ref, second)
    near_own[1].wait_recv()
    wide[1, "own"] = spread(shard(1, 0, own), second)
    near_far[1].wait_recv()
    ref = shard(1, 0, far)
    through_far = send(ref, ref, first[3])
    wide[1, "far"] = spread(ref, second)
    near_far[0].wait_recv()
    wide[3, "far"] = spread(shard(3, 0, far), second)

    passed = []

    def pass_on(d1):
        wide[d1, "own"][0].wait_recv()
        ref = shard(d1, 3, own)
        passed.append(send(ref, ref, second[1]))
        wide[d1, "far"][1].wait_recv()
        ref = shard(d1, 1, far)
        passed.append(send(ref, ref, second[3]))

    for copy in copy_z:
        copy.wait()

    def split_z(i, _):
        zh[i], zl[i] = split(z_in[i])
        return 0

    lax.fori_loop(0, 4, split_z, 0)

    pass_on(0)
    through_own.wait_recv()
    wide[2, "own"] = spread(shard(2, 0, own), second)
    through_far.wait_recv()
    wide[2, "far"] = spread(shard(2, 0, far), second)

    r_to_z.wait_recv()
    r_far = r4.at[2 * (1 - z_lo) + core]
    r_on = send(r_far, r_far, partner)
    pass_on(3)
    r_to_core.wait_recv()
    r_on.wait_recv()

    def split_r(i, _):
        rh[i], rl[i] = split(r4[i])
        return 0

    lax.fori_loop(0, 4, split_r, 0)

    def times_right(bh, bl):
        total = None
        for s in range(4):
            cols = slice(256 * s, 256 * s + 256)
            term = dot3(rh[s], rl[s], bh[:, cols], bl[:, cols], NT)
            total = term if total is None else total + term
        return total

    def mix(i, _):
        mh[i], ml[i] = split(times_right(zh.at[i], zl.at[i]))
        return 0

    mix(i2, 0)
    pass_on(1)
    mix(lax.rem(i2 + 3, 4), 0)
    mix(lax.rem(i2 + 1, 4), 0)

    def subtract(i):
        lth[i], ltl[i] = split(lt[i])
        for n in range(0, 1024, 256):
            cols = slice(n, n + 256)
            rest[:, cols] -= dot3(mh[i], ml[i], lth[i, :, cols], ltl[i, :, cols], NN)

    subtract(i2)
    pass_on(2)
    mix(lax.rem(i2 + 2, 4), 0)
    for d1 in range(4):
        wide[d1, "far"][0].wait_recv()
    subtract(lax.rem(i2 + 3, 4))
    for d1 in range(4):
        wide[d1, "own"][1].wait_recv()
    subtract(lax.rem(i2 + 1, 4))
    for copy in passed:
        copy.wait_recv()
    subtract(lax.rem(i2 + 2, 4))

    def split_rest(i, _):
        rows = pl.ds(aligned(128 * i, 128), 128)
        resh[rows, :], resl[rows, :] = split(rest[rows, :])
        return 0

    lax.fori_loop(0, 4, split_rest, 0)

    def project(yy):
        for i in range(2):
            parts = []
            for j in (2 * i, 2 * i + 1):
                at2, at1 = yy * other + j * core, j * other + yy * core
                rows = pl.ds(aligned(64 * at1, 64), 64)
                parts.append((lth[at2, rows, :], ltl[at2, rows, :]))
            ah = jnp.concatenate([p[0] for p in parts], axis=0)
            al = jnp.concatenate([p[1] for p in parts], axis=0)
            u[yy, 128 * i : 128 * i + 128, :] = dot3(ah, al, resh[...], resl[...], NT)

    u_sent = []
    for j in range(2):
        project(2 * other + j)
        u_sent.append(send(u.at[2 * other + j], u_in.at[j], partner))
    for j in range(2):
        project(2 * core + j)
    for j in range(2):
        u_sent[j].wait_recv()
        uh[256 * j : 256 * j + 256, :], ul[256 * j : 256 * j + 256, :] = split(u[2 * core + j] + u_in[j])

    def term(s):
        return dot3(uh[...], ul[...], rh[s], rl[s], NN)

    gp_a[:, :256] = term(0)
    second_part = term(1)
    gp_a[:, 256:] = second_part[:, :128]
    gp_b[:, :128] = second_part[:, 128:]
    gp_b[:, 128:] = term(2)
    gp_c[...] = term(3)

    def gradient(n0, w, order, gp, relay, ra, acc, rb, accb, rc):
        a, b, e = order
        ia, ib, ie = coord[a], coord[b], coord[e]
        cols = pl.ds(n0, w)
        opposite, after, before = (aligned(128 * lax.rem(ia + d, 4), 128) for d in (2, 1, 3))
        m1 = send(gp.at[pl.ds(opposite, 64), :], relay.at[0], peer[a][1])
        m2 = send(gp.at[pl.ds(aligned(opposite + 64, 64), 64), :], relay.at[1], peer[a][3])
        m3 = send(gp.at[pl.ds(aligned(after + 64, 64), 64), :], ra.at[0, pl.ds(64, 64), :], peer[a][1])
        m4 = send(gp.at[pl.ds(before, 64), :], ra.at[1, pl.ds(0, 64), :], peer[a][3])
        yield
        m1.wait_recv()
        rows = pl.ds(after, 64)
        gp[rows, :] += relay[0]
        m5 = send(gp.at[rows, :], ra.at[0, pl.ds(0, 64), :], peer[a][1])
        m2.wait_recv()
        rows = pl.ds(aligned(before + 64, 64), 64)
        gp[rows, :] += relay[1]
        m6 = send(gp.at[rows, :], ra.at[1, pl.ds(64, 64), :], peer[a][3])
        yield
        for m in (m3, m4, m5, m6):
            m.wait_recv()
        acc[...] = gp[pl.ds(aligned(128 * ia, 128), 128), :] + ra[0] + ra[1]
        ms = []
        for d in (1, 2, 3):
            rows = pl.ds(aligned(32 * lax.rem(ib + d, 4), 32), 32)
            ms.append(send(acc.at[rows, :], rb.at[d - 1], peer[b][d]))
        yield
        for m in ms:
            m.wait_recv()
        accb[...] = acc[pl.ds(aligned(32 * ib, 32), 32), :] + rb[0] + rb[1] + rb[2]
        ms = []
        for d in (1, 2, 3):
            rows = pl.ds(aligned(8 * lax.rem(ie + d, 4), 8), 8)
            ms.append(send(accb.at[rows, :], rc.at[d - 1], peer[e][d]))
        yield
        for m in ms:
            m.wait_recv()
        base = 512 * core + 128 * ia
        at = pl.ds(aligned(base + 32 * ib + 8 * ie, 8), 8)
        g[at, n0 : n0 + w] = accb[pl.ds(aligned(8 * ie, 8), 8), :] + rc[0] + rc[1] + rc[2]
        ms = [send(g.at[at, cols], g.at[at, cols], peer[e][d]) for d in (1, 2, 3)]
        yield
        for m in ms:
            m.wait_recv()
        at = pl.ds(aligned(base + 32 * ib, 32), 32)
        ms = [send(g.at[at, cols], g.at[at, cols], peer[b][d]) for d in (1, 2, 3)]
        yield
        for m in ms:
            m.wait_recv()
        at = g.at[pl.ds(aligned(base, 128), 128), cols]
        right, left = send(at, at, peer[a][1]), send(at, at, peer[a][3])
        over = [send(at, at, partner)]
        yield
        right.wait_recv()
        row = 512 * core + before
        at = g.at[pl.ds(aligned(row, 64), 64), cols]
        on_right = send(at, at, peer[a][1])
        at = g.at[pl.ds(aligned(row, 128), 128), cols]
        over.append(send(at, at, partner))
        left.wait_recv()
        row = 512 * core + after
        at = g.at[pl.ds(aligned(row + 64, 64), 64), cols]
        on_left = send(at, at, peer[a][3])
        at = g.at[pl.ds(aligned(row, 128), 128), cols]
        over.append(send(at, at, partner))
        yield
        on_right.wait_recv()
        on_left.wait_recv()
        at = g.at[pl.ds(aligned(512 * core + opposite, 128), 128), cols]
        over.append(send(at, at, partner))
        yield
        for m in over:
            m.wait_recv()

    buffers = (
        (gp_a, relay_a, ra_a, acc_a, rb_a, accb_a, rc_a),
        (gp_b, relay_b, ra_b, acc_b, rb_b, accb_b, rc_b),
        (gp_c, relay_c, ra_c, acc_c, rb_c, accb_c, rc_c),
    )
    lockstep(gradient(*group, *held) for group, held in zip(GROUPS, buffers))

    copy_g = pltpu.make_async_copy(g, g_hbm, local_sems.at[3])
    copy_g.start()

    rest[...] = jnp.zeros_like(rest)

    def image(i, _):
        for j in range(4):
            row = 64 * (i * (4 - 3 * core) + j * (1 + 3 * core))
            rows = slice(64 * j, 64 * j + 64)
            gch[rows, :], gcl[rows, :] = split(g[pl.ds(aligned(row, 64), 64), :])
        ih[...], il[...] = split(times_right(gch, gcl))
        for n in range(0, 1024, 256):
            cols = slice(n, n + 256)
            rest[:, cols] += dot3(ih[...], il[...], lth[i, :, cols], ltl[i, :, cols], NN)
        return 0

    lax.fori_loop(0, 4, image, 0)

    def squares(ref, rows_in_all):
        def body(i, total):
            part = ref[pl.ds(aligned(32 * i, 32), 32), :]
            part = part * part
            return total + jnp.sum(part.reshape(4, 8, 1024), axis=0)

        total = lax.fori_loop(0, rows_in_all // 32, body, jnp.zeros((8, 1024), F32))
        return functools.reduce(jnp.add, [total[:, 128 * i : 128 * i + 128] for i in range(8)])

    slots[3, core] = squares(rest, 512)
    ms = [send(slots.at[3, core], slots.at[3, core], partner)]
    numer = squares(g, 1024)
    for n, a in enumerate("xyz"):
        for m in ms:
            m.wait_recv()
        before = slots[3, 0] + slots[3, 1] if n == 0 else functools.reduce(jnp.add, [slots[n - 1, i] for i in range(4)])
        slots[n, coord[a]] = before
        at = slots.at[n, coord[a]]
        ms = [send(at, at, peer[a][d]) for d in (1, 2, 3)]
    for m in ms:
        m.wait_recv()
    denom = functools.reduce(jnp.add, [slots[2, i] for i in range(4)])
    total = lambda v: jnp.sum(jnp.sum(v, axis=0, keepdims=True), axis=1, keepdims=True)
    step_ref[...] = jnp.broadcast_to(total(numer) / total(denom), (8, 128))

    copy_g.wait()
    for copy in send.sent:
        copy.wait_send()


def scratch():
    v = pltpu.VMEM
    groups = [w for _, w, _ in GROUPS]
    return [
        v((1024, 32), F32), v((1024, 512), F32), v((4, 256, 1024), F32), v((4, 256, 1024), F32),
        v((4, 512, 256), F32), v((512, 1024), F32), v((4, 256, 512), F32), v((2, 256, 512), F32), v((1024, 1024), F32),
        v((4, 256, 1024), BF16), v((4, 256, 1024), BF16), v((4, 512, 256), BF16), v((4, 512, 256), BF16),
        v((4, 256, 1024), BF16), v((4, 256, 1024), BF16), v((4, 512, 256), BF16), v((4, 512, 256), BF16),
        v((512, 1024), BF16), v((512, 1024), BF16), v((512, 512), BF16), v((512, 512), BF16),
        v((256, 1024), BF16), v((256, 1024), BF16), v((512, 256), BF16), v((512, 256), BF16),
        *[v((512, w), F32) for w in groups], *[v((2, 64, w), F32) for w in groups],
        *[v((2, 128, w), F32) for w in groups], *[v((128, w), F32) for w in groups],
        *[v((3, 32, w), F32) for w in groups], *[v((32, w), F32) for w in groups],
        *[v((3, 8, w), F32) for w in groups],
        v((4, 4, 8, 128), F32),
        pltpu.SemaphoreType.DMA((MESSAGES,)), pltpu.SemaphoreType.DMA((MESSAGES,)), pltpu.SemaphoreType.DMA((20,)),
    ]


def shards(pair_integrals, left_factor, core, right_factor):
    gradient, step = pl.pallas_call(
        kernel,
        out_shape=(jax.ShapeDtypeStruct((1024, 1024), F32), jax.ShapeDtypeStruct((8, 128), F32)),
        in_specs=[pl.BlockSpec(memory_space=pl.ANY)] * 4,
        out_specs=(pl.BlockSpec(memory_space=pl.ANY), pl.BlockSpec(memory_space=pltpu.VMEM)),
        scratch_shapes=scratch(),
        compiler_params=pltpu.CompilerParams(
            collective_id=0, has_side_effects=True, vmem_limit_bytes=60 * 1024 * 1024
        ),
        cost_estimate=pl.CostEstimate(flops=7 * 10**9, bytes_accessed=16 * 2**20, transcendentals=0),
    )(pair_integrals, left_factor, core, right_factor)
    return core + step[0, 0] * gradient


def solution(mesh):
    placed = (P("rows", "cols"), P("rows", "cols"), P(), P("cols", "rows"))
    return jax.shard_map(shards, mesh=mesh, in_specs=placed, out_specs=P(), check_vma=False)
```

time: 384 us -> 125 us (0.33); the launches traced: 377 us -> 125 us
  waiting for transfers between devices: 201 us -> 0 us
  Pallas kernels: 0 us -> 114 us
  matrix products: 71.1 us -> 0 us
  blocking collectives: 67 us -> 0 us
  between operations: 15 us -> 0.01 us
  local copies, waits for them, and re-layouts: 12.2 us -> 3.17 us
    psum x1 -> x0, waiting for transfers between devices: 151 us -> none  [shards(): gradient = lax.psum(local_term, ROWS_COLS)]
    pallas_call x0 -> x1, Pallas kernels: none -> 114 us  [shards(): pl.pallas_call(kernel, out_shape=(jax.ShapeDtypeStruct((1024, 1024), F32)...]
    dot_general x6 -> x0, matrix products: 71.1 us -> none  [product(): jnp.dot(left, right, precision=lax.Precision.HIGHEST, preferred_element_t...]
    all_gather x1 -> x0, waiting for transfers between devices: 48.8 us -> none  [shards(): left_rows = lax.all_gather(left_factor, COLS, axis=1, tiled=True)]
    psum x5 -> x0, blocking collectives: 37.1 us -> none  [one_axis_at_a_time(): return functools.reduce(lax.psum, axes, x)]
    all_to_all x1 -> x0, blocking collectives: 30 us -> none  [copy_for_each(): lax.all_to_all(jnp.broadcast_to(x[None], (devices, *x.shape)), axis, 0, 0...]
    add x1 -> x0, local copies, waits for them, and re-layouts: 5.34 us -> none  [shards(): return core + numer / denom * gradient]
    unnamed x10 -> x1, local copies, waits for them, and re-layouts: 6.59 us -> 1.9 us
  transfers between devices with their start and end apart: 2 -> 0, of which waited for: 2 -> 0; matrix products, arithmetic and copies ran while one was open for 3% -> 0% of each run, Pallas kernels for 0% -> 0%
where the time goes in v1:
time: 125 us
  Pallas kernels  114 us (91%)
  other arithmetic  7.6 us (6%)
  local copies, waits for them, and re-layouts  3.17 us (3%)
    pallas_call x1, Pallas kernels, shards(): pl.pallas_call(kernel, out_shape=(jax.ShapeDtypeStruct((1024, 1024), F32)...  114 us
    add x1, other arithmetic, shards(): return core + step[0, 0] * gradient  7.6 us

profile of v1, /device:TPU:0, one launch (start us, length us, event | category | flops | bytes accessed | tf_op | source)
XLA Modules:
  0.0 124.8 jit_solution(13244998182434687243)
XLA Ops:
  0.0 1.9 %copy.5.l_hbm = f32[1024,32]{1,0:T(8,128)} copy(f32[1024,32]{0,1:T(8,128)} %param.5) | data formatting | bytes 262144 | tf_op args[1]
  1.9 114.0 %shard_map.46 = (f32[1024,1024]{1,0:T(8,128)}, f32[8,128]{1,0:T(8,128)}) custom-call(f32[1024,512]{1,0:T(8,128)} %v_hbm.1, f32[1024,32]{1,0:T(8,128)} %copy.5.l_hbm, f32[1024,1024]{1,0:T(8,128)} %z_hbm.1, f32[512,256]{1,0:T(8,128)} %r_hbm.1), custom_call_target="tpu_custom_call" | custom-call | flops 7000000000 | bytes 16777216 | tf_op jit(solution)/shard_map/pallas_call | solution.py:428
  115.9 1.3 %slice.3 = f32[1,1]{1,0:T(1,128)} slice(f32[8,128]{1,0:T(8,128)} %get-tuple-element.7), slice={[0:1], [0:1]} | slice | bytes 8 | tf_op jit(solution)/shard_map/slice | solution.py:439
  117.2 7.6 %multiply_add_fusion = f32[1024,1024]{1,0:T(8,128)} fusion(f32[1024,1024]{1,0:T(8,128)} %z_hbm.1, f32[1024,1024]{1,0:T(8,128)} %get-tuple-element.8, f32[]{:T(128)} %bitcast), kind=kLoop, calls=%fused_computation | loop fusion | flops 2097152 | bytes 12582916 | tf_op jit(solution)/shard_map/add | solution.py:439

commit v2 on v1

--- a/solution.py
+++ b/solution.py
@@ -21,8 +21,13 @@
 
 
 def dot3(ah, al, bh, bl, dims):
-    dot = functools.partial(lax.dot_general, dimension_numbers=dims, preferred_element_type=F32)
-    return dot(ah, bh) + dot(ah, bl) + dot(al, bh)
+    (da,), (db,) = dims[0]
+    return lax.dot_general(
+        jnp.concatenate([ah, ah, al], da),
+        jnp.concatenate([bh, bl, bh], db),
+        dimension_numbers=dims,
+        preferred_element_type=F32,
+    )
 
 
 def aligned(i, m):
@@ -62,8 +67,8 @@
 
 
 def kernel(
-    v_hbm, l_hbm, z_hbm, r_hbm, g_hbm, step_ref,
-    l_in, v_in, z_in, lt, r4, rest, u, u_in, g,
+    v_hbm, l_hbm, z_hbm, r_hbm, out,
+    v_in, z_in, lt, r4, rest, u, u_in, g,
     zh, zl, rh, rl, lth, ltl, mh, ml, resh, resl, uh, ul, gch, gcl, ih, il,
     gp_a, gp_b, gp_c, relay_a, relay_b, relay_c, ra_a, ra_b, ra_c,
     acc_a, acc_b, acc_c, rb_a, rb_b, rb_c, accb_a, accb_b, accb_c, rc_a, rc_b, rc_c,
@@ -91,7 +96,8 @@
     second = [device(d * core, d * other, 0, core) for d in range(4)]
     i1, i2 = x * other + y * core, y * other + x * core
 
-    copy_l = pltpu.make_async_copy(l_hbm, l_in, local_sems.at[0])
+    at_l = (i2, pl.ds(aligned(64 * i1 + 32 * z_hi, 32), 32))
+    copy_l = pltpu.make_async_copy(l_hbm, lt.at[at_l], local_sems.at[0])
     copy_r = pltpu.make_async_copy(r_hbm, r4.at[r], local_sems.at[1])
     copy_v = pltpu.make_async_copy(v_hbm, v_in, local_sems.at[2])
     copy_l.start()
@@ -127,7 +133,6 @@
 
     own, far = z_hi, 1 - z_hi
     copy_l.wait()
-    lt[i2, pl.ds(aligned(64 * i1 + 32 * own, 32), 32), :] = jnp.transpose(l_in[...])
     mine = shard(0, 0, own)
     to_z = send(mine, mine, z_hi_partner)
     near_own = spread(mine, first)
@@ -196,22 +201,17 @@
     r_to_core.wait_recv()
     r_on.wait_recv()
 
-    def split_r(i, _):
-        rh[i], rl[i] = split(r4[i])
-        return 0
-
-    lax.fori_loop(0, 4, split_r, 0)
-
-    def times_right(bh, bl):
-        total = None
-        for s in range(4):
-            cols = slice(256 * s, 256 * s + 256)
-            term = dot3(rh[s], rl[s], bh[:, cols], bl[:, cols], NT)
-            total = term if total is None else total + term
-        return total
+    for i in range(4):
+        cols = slice(256 * i, 256 * i + 256)
+        rh[:, cols], rl[:, cols] = split(r4[i])
+
+    def times_right(m, bh, bl):
+        rows = slice(m, m + 256)
+        return split(dot3(rh[rows, :], rl[rows, :], bh[...], bl[...], NT))
 
     def mix(i, _):
-        mh[i], ml[i] = split(times_right(zh.at[i], zl.at[i]))
+        for m in (0, 256):
+            mh[i, m : m + 256, :], ml[i, m : m + 256, :] = times_right(m, zh.at[i], zl.at[i])
         return 0
 
     mix(i2, 0)
@@ -246,15 +246,14 @@
     lax.fori_loop(0, 4, split_rest, 0)
 
     def project(yy):
-        for i in range(2):
-            parts = []
-            for j in (2 * i, 2 * i + 1):
-                at2, at1 = yy * other + j * core, j * other + yy * core
-                rows = pl.ds(aligned(64 * at1, 64), 64)
-                parts.append((lth[at2, rows, :], ltl[at2, rows, :]))
-            ah = jnp.concatenate([p[0] for p in parts], axis=0)
-            al = jnp.concatenate([p[1] for p in parts], axis=0)
-            u[yy, 128 * i : 128 * i + 128, :] = dot3(ah, al, resh[...], resl[...], NT)
+        parts = []
+        for j in range(4):
+            at2, at1 = yy * other + j * core, j * other + yy * core
+            rows = pl.ds(aligned(64 * at1, 64), 64)
+            parts.append((lth[at2, rows, :], ltl[at2, rows, :]))
+        ah = jnp.concatenate([p[0] for p in parts], axis=0)
+        al = jnp.concatenate([p[1] for p in parts], axis=0)
+        u[yy] = dot3(ah, al, resh[...], resl[...], NT)
 
     u_sent = []
     for j in range(2):
@@ -266,15 +265,20 @@
         u_sent[j].wait_recv()
         uh[256 * j : 256 * j + 256, :], ul[256 * j : 256 * j + 256, :] = split(u[2 * core + j] + u_in[j])
 
-    def term(s):
-        return dot3(uh[...], ul[...], rh[s], rl[s], NN)
-
-    gp_a[:, :256] = term(0)
-    second_part = term(1)
-    gp_a[:, 256:] = second_part[:, :128]
-    gp_b[:, :128] = second_part[:, 128:]
-    gp_b[:, 128:] = term(2)
-    gp_c[...] = term(3)
+    for m in (0, 256):
+        rows = slice(m, m + 256)
+        for s in range(4):
+            cols = slice(256 * s, 256 * s + 256)
+            term = dot3(uh[rows, :], ul[rows, :], rh[:, cols], rl[:, cols], NN)
+            if s == 0:
+                gp_a[rows, :256] = term
+            elif s == 1:
+                gp_a[rows, 256:] = term[:, :128]
+                gp_b[rows, :128] = term[:, 128:]
+            elif s == 2:
+                gp_b[rows, 128:] = term
+            else:
+                gp_c[rows, :] = term
 
     def gradient(n0, w, order, gp, relay, ra, acc, rb, accb, rc):
         a, b, e = order
@@ -357,9 +361,6 @@
     )
     lockstep(gradient(*group, *held) for group, held in zip(GROUPS, buffers))
 
-    copy_g = pltpu.make_async_copy(g, g_hbm, local_sems.at[3])
-    copy_g.start()
-
     rest[...] = jnp.zeros_like(rest)
 
     def image(i, _):
@@ -367,7 +368,8 @@
             row = 64 * (i * (4 - 3 * core) + j * (1 + 3 * core))
             rows = slice(64 * j, 64 * j + 64)
             gch[rows, :], gcl[rows, :] = split(g[pl.ds(aligned(row, 64), 64), :])
-        ih[...], il[...] = split(times_right(gch, gcl))
+        for m in (0, 256):
+            ih[m : m + 256, :], il[m : m + 256, :] = times_right(m, gch, gcl)
         for n in range(0, 1024, 256):
             cols = slice(n, n + 256)
             rest[:, cols] += dot3(ih[...], il[...], lth[i, :, cols], ltl[i, :, cols], NN)
@@ -398,9 +400,17 @@
         m.wait_recv()
     denom = functools.reduce(jnp.add, [slots[2, i] for i in range(4)])
     total = lambda v: jnp.sum(jnp.sum(v, axis=0, keepdims=True), axis=1, keepdims=True)
-    step_ref[...] = jnp.broadcast_to(total(numer) / total(denom), (8, 128))
-
-    copy_g.wait()
+    step = total(numer) / total(denom)
+
+    def update(b, _):
+        by, bx = lax.div(b, 4), lax.rem(b, 4)
+        at2, at1 = by * other + bx * core, bx * other + by * core
+        rows = pl.ds(aligned(64 * b, 64), 64)
+        out[rows, :] = z_in[at2, pl.ds(aligned(64 * at1, 64), 64), :] + step * g[rows, :]
+        return 0
+
+    lax.fori_loop(0, 16, update, 0)
+
     for copy in send.sent:
         copy.wait_send()
 
@@ -409,9 +419,9 @@
     v = pltpu.VMEM
     groups = [w for _, w, _ in GROUPS]
     return [
-        v((1024, 32), F32), v((1024, 512), F32), v((4, 256, 1024), F32), v((4, 256, 1024), F32),
+        v((1024, 512), F32), v((4, 256, 1024), F32), v((4, 256, 1024), F32),
         v((4, 512, 256), F32), v((512, 1024), F32), v((4, 256, 512), F32), v((2, 256, 512), F32), v((1024, 1024), F32),
-        v((4, 256, 1024), BF16), v((4, 256, 1024), BF16), v((4, 512, 256), BF16), v((4, 512, 256), BF16),
+        v((4, 256, 1024), BF16), v((4, 256, 1024), BF16), v((512, 1024), BF16), v((512, 1024), BF16),
         v((4, 256, 1024), BF16), v((4, 256, 1024), BF16), v((4, 512, 256), BF16), v((4, 512, 256), BF16),
         v((512, 1024), BF16), v((512, 1024), BF16), v((512, 512), BF16), v((512, 512), BF16),
         v((256, 1024), BF16), v((256, 1024), BF16), v((512, 256), BF16), v((512, 256), BF16),
@@ -425,18 +435,18 @@
 
 
 def shards(pair_integrals, left_factor, core, right_factor):
-    gradient, step = pl.pallas_call(
+    in_hbm = functools.partial(pltpu.with_memory_space_constraint, memory_space=pltpu.HBM)
+    return pl.pallas_call(
         kernel,
-        out_shape=(jax.ShapeDtypeStruct((1024, 1024), F32), jax.ShapeDtypeStruct((8, 128), F32)),
-        in_specs=[pl.BlockSpec(memory_space=pl.ANY)] * 4,
-        out_specs=(pl.BlockSpec(memory_space=pl.ANY), pl.BlockSpec(memory_space=pltpu.VMEM)),
+        out_shape=pltpu.VMEM((1024, 1024), F32),
+        in_specs=[pl.BlockSpec(memory_space=pltpu.HBM)] * 4,
+        out_specs=pl.BlockSpec(memory_space=pltpu.VMEM),
         scratch_shapes=scratch(),
         compiler_params=pltpu.CompilerParams(
-            collective_id=0, has_side_effects=True, vmem_limit_bytes=60 * 1024 * 1024
+            collective_id=0, has_side_effects=True, vmem_limit_bytes=54 * 1024 * 1024
         ),
         cost_estimate=pl.CostEstimate(flops=7 * 10**9, bytes_accessed=16 * 2**20, transcendentals=0),
-    )(pair_integrals, left_factor, core, right_factor)
-    return core + step[0, 0] * gradient
+    )(*map(in_hbm, (pair_integrals, left_factor.T, core, right_factor)))
 
 
 def solution(mesh):

time: 125 us -> 103 us (0.82)
  Pallas kernels: 114 us -> 101 us
  other arithmetic: 7.6 us -> 0 us
    pallas_call x1, Pallas kernels: 114 us -> 101 us  [shards(): pl.pallas_call(kernel, out_shape=pltpu.VMEM((1024, 1024), F32), in_specs=...]
    add x1 -> x0, other arithmetic: 7.6 us -> none  [shards(): return core + step[0, 0] * gradient]
    slice x1 -> x0, local copies, waits for them, and re-layouts: 1.26 us -> none  [shards(): return core + step[0, 0] * gradient]
where the time goes in v2:
time: 103 us
  Pallas kernels  101 us (98%)
  local copies, waits for them, and re-layouts  2.02 us (2%)
    pallas_call x1, Pallas kernels, shards(): pl.pallas_call(kernel, out_shape=pltpu.VMEM((1024, 1024), F32), in_specs=...  101 us

profile of v2, /device:TPU:0, one launch (start us, length us, event | category | flops | bytes accessed | tf_op | source)
XLA Modules:
  0.0 102.8 jit_solution(7622075902701455647)
XLA Ops:
  0.0 100.8 %shard_map.46 = f32[1024,1024]{1,0:T(8,128)S(1)} custom-call(f32[1024,512]{1,0:T(8,128)} %v_hbm.1, f32[32,1024]{1,0:T(8,128)} %bitcast.1, f32[1024,1024]{1,0:T(8,128)} %z_hbm.1, f32[512,256]{1,0:T(8,128)} %r_hbm.1), custom_call_target="tpu_custom_call" | custom-call | flops 7000000000 | bytes 16777216 | tf_op jit(solution)/shard_map/pallas_call | solution.py:439
  100.8 2.0 %copy.6 = f32[1024,1024]{1,0:T(8,128)} copy(f32[1024,1024]{1,0:T(8,128)S(1)} %shard_map.46) | data formatting | bytes 8388608

commit v3 on v2

v3 whole, which is shorter than its diff:
```python
import functools

import jax
import jax.numpy as jnp
from jax import lax
from jax.experimental import pallas as pl
from jax.experimental.pallas import tpu as pltpu
from jax.sharding import PartitionSpec as P

MESH = pl.DeviceIdType.MESH
F32, BF16 = jnp.float32, jnp.bfloat16
GROUPS = ((0, 256), (256, 128), (384, 128))
MESSAGES = 160
NN = (((1,), (0,)), ((), ()))
NT = (((1,), (1,)), ((), ()))


def split(v):
    hi = v.astype(BF16)
    return hi, (v - hi.astype(F32)).astype(BF16)


def dot3(ah, al, bh, bl, dims):
    (da,), (db,) = dims[0]
    return lax.dot_general(
        jnp.concatenate([ah, ah, al], da),
        jnp.concatenate([bh, bl, bh], db),
        dimension_numbers=dims,
        preferred_element_type=F32,
    )


def aligned(i, m):
    return pl.multiple_of(i, m)


class Sender:
    def __init__(self, send_sems, recv_sems):
        self.send_sems, self.recv_sems, self.sent = send_sems, recv_sems, []

    def __call__(self, src, dst, peer):
        i = len(self.sent)
        copy = pltpu.make_async_remote_copy(
            src_ref=src,
            dst_ref=dst,
            send_sem=self.send_sems.at[i],
            recv_sem=self.recv_sems.at[i],
            device_id=peer,
            device_id_type=MESH,
        )
        copy.start()
        self.sent.append(copy)
        return copy


def lockstep(generators):
    live = list(generators)
    while live:
        still = []
        for g in live:
            try:
                next(g)
                still.append(g)
            except StopIteration:
                pass
        live = still


def kernel(
    v_hbm, l_hbm, z_hbm, r_hbm, out,
    v_in, z_in, lt, r4, rest, u, u_in, g,
    zh, zl, rh, rl, lth, ltl, mh, ml, resh, resl, uh, ul, inner, ih, il,
    gp, relay, ra, acc, rb, ring, slots_z, slots_xy, send_sems, recv_sems, local_sems,
):
    r, c = lax.axis_index("rows"), lax.axis_index("cols")
    core, z_lo, z_hi = lax.rem(r, 2), lax.div(r, 2), lax.rem(c, 2)
    x, y, z = lax.rem(lax.div(c, 2), 4), lax.div(c, 8), 2 * z_hi + z_lo
    other = 1 - core

    def device(dx, dy, dz, k):
        xx, yy, zz = lax.rem(x + dx, 4), lax.rem(y + dy, 4), lax.rem(z + dz, 4)
        return (2 * lax.rem(zz, 2) + k, 8 * yy + 2 * xx + lax.div(zz, 2))

    partner = device(0, 0, 0, other)
    z_lo_partner = (2 * (1 - z_lo) + core, c)
    z_hi_partner = device(0, 0, 2, core)
    near_z = [device(0, 0, d, k) for d in range(4) for k in (core, other)][1:]
    near_xy = [device(dx, dy, 0, core) for dx in range(4) for dy in range(4)][1:]
    first = [device(d * other, d * core, 0, core) for d in range(4)]
    second = [device(d * core, d * other, 0, core) for d in range(4)]
    i1, i2 = x * other + y * core, y * other + x * core

    at_l = (i2, pl.ds(aligned(64 * i1 + 32 * z_hi, 32), 32))
    copy_l = pltpu.make_async_copy(l_hbm, lt.at[at_l], local_sems.at[0])
    copy_r = pltpu.make_async_copy(r_hbm, r4.at[r], local_sems.at[1])
    copy_v = pltpu.make_async_copy(v_hbm, v_in, local_sems.at[2])
    copy_l.start()
    copy_r.start()
    copy_v.start()
    copy_z = []
    for b in range(16):
        by, bx = b // 4, b % 4
        at2, at1 = by * other + bx * core, bx * other + by * core
        copy_z.append(
            pltpu.make_async_copy(
                z_hbm.at[pl.ds(64 * b, 64), :],
                z_in.at[at2, pl.ds(aligned(64 * at1, 64), 64), :],
                local_sems.at[4 + b],
            )
        )
        copy_z[-1].start()

    barrier = pltpu.get_barrier_semaphore()
    greeted = near_z + near_xy
    for other_device in greeted:
        pl.semaphore_signal(barrier, inc=1, device_id=other_device, device_id_type=MESH)
    pl.semaphore_wait(barrier, len(greeted))

    send = Sender(send_sems, recv_sems)

    def shard(d1, d2, h):
        at1, at2 = lax.rem(i1 + d1, 4), lax.rem(i2 + d2, 4)
        return lt.at[at2, pl.ds(aligned(64 * at1 + 32 * h, 32), 32), :]

    def spread(ref, peers):
        return send(ref, ref, peers[1]), send(ref, ref, peers[3])

    own, far = z_hi, 1 - z_hi
    copy_l.wait()
    mine = shard(0, 0, own)
    to_z = send(mine, mine, z_hi_partner)
    near_own = spread(mine, first)
    wide = {(0, "own"): spread(mine, second)}

    copy_r.wait()
    r_to_core = send(r4.at[r], r4.at[r], partner)
    r_to_z = send(r4.at[r], r4.at[r], z_lo_partner)

    def transpose_v(i):
        rest[:, 128 * i : 128 * i + 128] = jnp.transpose(v_in[128 * i : 128 * i + 128, :])

    copy_v.wait()
    for i in range(4):
        transpose_v(i)

    to_z.wait_recv()
    theirs = shard(0, 0, far)
    near_far = spread(theirs, first)
    wide[0, "far"] = spread(theirs, second)
    for i in range(4, 8):
        transpose_v(i)

    near_own[0].wait_recv()
    ref = shard(3, 0, own)
    through_own = send(ref, ref, first[1])
    wide[3, "own"] = spread(ref, second)
    near_own[1].wait_recv()
    wide[1, "own"] = spread(shard(1, 0, own), second)
    near_far[1].wait_recv()
    ref = shard(1, 0, far)
    through_far = send(ref, ref, first[3])
    wide[1, "far"] = spread(ref, second)
    near_far[0].wait_recv()
    wide[3, "far"] = spread(shard(3, 0, far), second)

    passed = []

    def pass_on(d1):
        wide[d1, "own"][0].wait_recv()
        ref = shard(d1, 3, own)
        passed.append(send(ref, ref, second[1]))
        wide[d1, "far"][1].wait_recv()
        ref = shard(d1, 1, far)
        passed.append(send(ref, ref, second[3]))

    pass_on(0)
    through_own.wait_recv()
    wide[2, "own"] = spread(shard(2, 0, own), second)
    through_far.wait_recv()
    wide[2, "far"] = spread(shard(2, 0, far), second)

    for copy in copy_z:
        copy.wait()

    def split_z(i, _):
        zh[i], zl[i] = split(z_in[i])
        return 0

    lax.fori_loop(0, 4, split_z, 0)
    pass_on(3)
    pass_on(1)

    r_to_z.wait_recv()
    r_far = r4.at[2 * (1 - z_lo) + core]
    r_on = send(r_far, r_far, partner)
    r_to_core.wait_recv()
    r_on.wait_recv()

    def split_r(i, _):
        rh[i], rl[i] = split(r4[i])
        return 0

    lax.fori_loop(0, 4, split_r, 0)

    def mix(i, _):
        for m in (0, 256):
            rows = slice(m, m + 256)
            ah, al = (jnp.concatenate([ref[k, rows, :] for k in range(4)], 1) for ref in (rh, rl))
            mh[i, rows, :], ml[i, rows, :] = split(dot3(ah, al, zh[i], zl[i], NT))
        return 0

    mix(i2, 0)
    mix(lax.rem(i2 + 3, 4), 0)

    def subtract(i):
        lth[i], ltl[i] = split(lt[i])
        for n in range(0, 1024, 256):
            cols = slice(n, n + 256)
            rest[:, cols] -= dot3(mh[i], ml[i], lth[i, :, cols], ltl[i, :, cols], NN)

    pass_on(2)
    mix(lax.rem(i2 + 1, 4), 0)
    mix(lax.rem(i2 + 2, 4), 0)
    subtract(i2)
    for d1 in range(4):
        wide[d1, "far"][0].wait_recv()
    subtract(lax.rem(i2 + 3, 4))
    for d1 in range(4):
        wide[d1, "own"][1].wait_recv()
    subtract(lax.rem(i2 + 1, 4))
    for copy in passed:
        copy.wait_recv()
    subtract(lax.rem(i2 + 2, 4))

    def split_rest(i, _):
        rows = pl.ds(aligned(128 * i, 128), 128)
        resh[rows, :], resl[rows, :] = split(rest[rows, :])
        return 0

    lax.fori_loop(0, 4, split_rest, 0)

    def rank_rows(yy):
        parts = []
        for j in range(4):
            at2, at1 = yy * other + j * core, j * other + yy * core
            rows = pl.ds(aligned(64 * at1, 64), 64)
            parts.append((lth[at2, rows, :], ltl[at2, rows, :]))
        return (jnp.concatenate([p[i] for p in parts], axis=0) for i in (0, 1))

    def project(yy):
        ah, al = rank_rows(yy)
        u[yy] = dot3(ah, al, resh[...], resl[...], NT)

    u_sent = []
    for j in range(2):
        project(2 * other + j)
        u_sent.append(send(u.at[2 * other + j], u_in.at[j], partner))
    for j in range(2):
        project(2 * core + j)
    for j in range(2):
        u_sent[j].wait_recv()
        uh[256 * j : 256 * j + 256, :], ul[256 * j : 256 * j + 256, :] = split(u[2 * core + j] + u_in[j])

    def gradient(n0, w, a, b, e, relay, ra, acc, rb, ring):
        half = w // 2
        ia, ib, ie = (x * v[0] + y * v[1] + z * v[2] for v in (a, b, e))
        towards = lambda v, d: device(d * v[0], d * v[1], d * v[2], core)
        opposite, after, before = (lax.rem(ia + d, 4) for d in (2, 1, 3))
        rows, top, low = pl.ds(n0, w), pl.ds(n0, half), pl.ds(n0 + half, half)

        def term(j):
            gp[j, rows, :] = dot3(uh[rows, :], ul[rows, :], rh[j], rl[j], NN)

        term(opposite)
        m1 = send(gp.at[opposite, top], relay.at[0], towards(a, 1))
        m2 = send(gp.at[opposite, low], relay.at[1], towards(a, 3))
        yield
        term(after)
        m3 = send(gp.at[after, low], ra.at[0, pl.ds(half, half)], towards(a, 1))
        term(before)
        m4 = send(gp.at[before, top], ra.at[1, pl.ds(0, half)], towards(a, 3))
        yield
        m1.wait_recv()
        gp[after, top, :] += relay[0]
        m5 = send(gp.at[after, top], ra.at[0, pl.ds(0, half)], towards(a, 1))
        m2.wait_recv()
        gp[before, low, :] += relay[1]
        m6 = send(gp.at[before, low], ra.at[1, pl.ds(half, half)], towards(a, 3))
        yield
        term(ia)
        yield
        for m in (m3, m4, m5, m6):
            m.wait_recv()
        acc[...] = gp[ia, rows, :] + ra[0] + ra[1]
        quarter = w // 4
        ms = []
        for d in (1, 2, 3):
            part = pl.ds(aligned(quarter * lax.rem(ib + d, 4), quarter), quarter)
            ms.append(send(acc.at[part], rb.at[d - 1], towards(b, d)))
        yield
        for m in ms:
            m.wait_recv()
        ring[ie] = acc[pl.ds(aligned(quarter * ib, quarter), quarter), :] + rb[0] + rb[1] + rb[2]
        ms = [send(ring.at[ie], ring.at[ie], towards(e, d)) for d in (1, 2, 3)]
        yield
        for m in ms:
            m.wait_recv()
        base = 512 * core + n0
        part = pl.ds(aligned(base + quarter * ib, quarter), quarter)
        g[ia, part, :] = ring[0] + ring[1] + ring[2] + ring[3]
        ms = [send(g.at[ia, part], g.at[ia, part], towards(b, d)) for d in (1, 2, 3)]
        yield
        for m in ms:
            m.wait_recv()
        rows, top, low = (pl.ds(aligned(base + i, half), n) for i, n in ((0, w), (0, half), (half, half)))
        right = send(g.at[ia, rows], g.at[ia, rows], towards(a, 1))
        left = send(g.at[ia, rows], g.at[ia, rows], towards(a, 3))

        def inner_part(j, start):
            bh, bl = split(g[j, rows, :])
            chunk, cols = n0 // 256, pl.ds(n0 % 256, w)
            for m in (0, 256):
                at = slice(m, m + 256)
                part = dot3(rh[j, at, :], rl[j, at, :], bh, bl, NT)
                inner[0, chunk, at, cols] = part if start else inner[0, chunk, at, cols] + part

        yield
        inner_part(ia, True)
        yield
        right.wait_recv()
        on_right = send(g.at[before, top], g.at[before, top], towards(a, 1))
        left.wait_recv()
        on_left = send(g.at[after, low], g.at[after, low], towards(a, 3))
        yield
        inner_part(before, False)
        inner_part(after, False)
        yield
        on_right.wait_recv()
        on_left.wait_recv()
        inner_part(opposite, False)

    xs, ys, zs = (1, 0, 0), (0, 1, 0), (0, 0, 1)
    orders = (
        ((other, core, 0), (0, other, core), (core, 0, other)),
        ((core, other, 0), (0, core, other), (other, 0, core)),
        (zs, xs, ys),
    )
    groups = [
        gradient(*group, *order, *(held[i] for held in (relay, ra, acc, rb, ring)))
        for i, (group, order) in enumerate(zip(GROUPS, orders))
    ]
    lockstep(groups)
    inner_sent = [send(inner.at[0, i], inner.at[1, i], partner) for i in range(2)]
    g_half = g.at[:, pl.ds(aligned(512 * core, 512), 512)]
    g_sent = send(g_half, g_half, partner)

    def image(side, i, yy):
        for m in (0, 256):
            rows = slice(m, m + 256)
            ih[rows, :], il[rows, :] = split(inner[side, i, rows, :])
        bh, bl = rank_rows(yy)
        for n in range(0, 1024, 256):
            cols = slice(n, n + 256)
            part = dot3(ih[...], il[...], bh[:, cols], bl[:, cols], NN)
            rest[:, cols] = part if (side, i) == (0, 0) else rest[:, cols] + part

    for i in range(2):
        image(0, i, 2 * core + i)
    for i in range(2):
        inner_sent[i].wait_recv()
        image(1, i, 2 * other + i)

    def fold(v):
        return functools.reduce(jnp.add, [v[:, i : i + 128] for i in range(0, v.shape[1], 128)])

    def squares(load, steps):
        def body(i, total):
            v = load(i)
            return total + jnp.sum((v * v).reshape(-1, 8, v.shape[1]), axis=0)

        return fold(lax.fori_loop(0, steps, body, jnp.zeros_like(load(0)[:8, :])))

    def share(value, slots, at, peers):
        slots[at] = value
        return [send(slots.at[at], slots.at[at], p) for p in peers]

    def gathered(messages, slots):
        for m in messages:
            m.wait_recv()
        return functools.reduce(jnp.add, [slots[i] for i in range(slots.shape[0])])

    denom = squares(lambda i: rest[pl.ds(aligned(32 * i, 32), 32), :], 16)
    messages = share(denom, slots_z, 2 * z + core, near_z)
    g_sent.wait_recv()
    numer = squares(lambda i: g[lax.div(i, 8), pl.ds(aligned(128 * lax.rem(i, 8), 128), 128), :], 32)
    messages = share(gathered(messages, slots_z), slots_xy, 4 * y + x, near_xy)
    denom = gathered(messages, slots_xy)
    total = lambda v: jnp.sum(jnp.sum(v, axis=0, keepdims=True), axis=1, keepdims=True)
    step = total(numer) / total(denom)

    def update(b, _):
        by, bx = lax.div(b, 4), lax.rem(b, 4)
        at2, at1 = by * other + bx * core, bx * other + by * core
        rows, from_rows = pl.ds(aligned(64 * b, 64), 64), pl.ds(aligned(64 * at1, 64), 64)
        for j in range(4):
            cols = slice(256 * j, 256 * j + 256)
            out[rows, cols] = z_in[at2, from_rows, cols] + step * g[j, rows, :]
        return 0

    lax.fori_loop(0, 16, update, 0)

    for copy in send.sent:
        copy.wait_send()


def scratch():
    v = pltpu.VMEM
    rows = [w for _, w in GROUPS]
    return [
        v((1024, 512), F32), v((4, 256, 1024), F32), v((4, 256, 1024), F32),
        v((4, 512, 256), F32), v((512, 1024), F32), v((4, 256, 512), F32), v((2, 256, 512), F32), v((4, 1024, 256), F32),
        v((4, 256, 1024), BF16), v((4, 256, 1024), BF16), v((4, 512, 256), BF16), v((4, 512, 256), BF16),
        v((4, 256, 1024), BF16), v((4, 256, 1024), BF16), v((4, 512, 256), BF16), v((4, 512, 256), BF16),
        v((512, 1024), BF16), v((512, 1024), BF16), v((512, 512), BF16), v((512, 512), BF16),
        v((2, 2, 512, 256), F32), v((512, 256), BF16), v((512, 256), BF16),
        v((4, 512, 256), F32), [v((2, w // 2, 256), F32) for w in rows], [v((2, w, 256), F32) for w in rows],
        [v((w, 256), F32) for w in rows], [v((3, w // 4, 256), F32) for w in rows],
        [v((4, w // 4, 256), F32) for w in rows],
        v((8, 8, 128), F32), v((16, 8, 128), F32),
        pltpu.SemaphoreType.DMA((MESSAGES,)), pltpu.SemaphoreType.DMA((MESSAGES,)), pltpu.SemaphoreType.DMA((20,)),
    ]


def shards(pair_integrals, left_factor, core, right_factor):
    in_hbm = functools.partial(pltpu.with_memory_space_constraint, memory_space=pltpu.HBM)
    return pl.pallas_call(
        kernel,
        out_shape=pltpu.VMEM((1024, 1024), F32),
        in_specs=[pl.BlockSpec(memory_space=pltpu.HBM)] * 4,
        out_specs=pl.BlockSpec(memory_space=pltpu.VMEM),
        scratch_shapes=scratch(),
        compiler_params=pltpu.CompilerParams(
            collective_id=0, has_side_effects=True, vmem_limit_bytes=54 * 1024 * 1024
        ),
        cost_estimate=pl.CostEstimate(flops=7 * 10**9, bytes_accessed=16 * 2**20, transcendentals=0),
    )(*map(in_hbm, (pair_integrals, left_factor.T, core, right_factor)))


def solution(mesh):
    placed = (P("rows", "cols"), P("rows", "cols"), P(), P("cols", "rows"))
    return jax.shard_map(shards, mesh=mesh, in_specs=placed, out_specs=P(), check_vma=False)
```

time: 103 us -> 97.3 us (0.945)
  Pallas kernels: 101 us -> 95 us
    pallas_call x1, Pallas kernels: 101 us -> 95 us  [shards(): pl.pallas_call(kernel, out_shape=pltpu.VMEM((1024, 1024), F32), in_specs=...]
where the time goes in v3:
time: 97.3 us; the launch traced here: 97 us
  Pallas kernels  95 us (98%)
  local copies, waits for them, and re-layouts  2.02 us (2%)
    pallas_call x1, Pallas kernels, shards(): pl.pallas_call(kernel, out_shape=pltpu.VMEM((1024, 1024), F32), in_specs=...  95 us
    unnamed x1, local copies, waits for them, and re-layouts  2.02 us

profile of v3, /device:TPU:0, one launch (start us, length us, event | category | flops | bytes accessed | tf_op | source)
XLA Modules:
  0.0 97.0 jit_solution(7523969566442725619)
XLA Ops:
  0.0 95.0 %shard_map.46 = f32[1024,1024]{1,0:T(8,128)S(1)} custom-call(f32[1024,512]{1,0:T(8,128)} %v_hbm.1, f32[32,1024]{1,0:T(8,128)} %bitcast.1, f32[1024,1024]{1,0:T(8,128)} %z_hbm.1, f32[512,256]{1,0:T(8,128)} %r_hbm.1), custom_call_target="tpu_custom_call" | custom-call | flops 7000000000 | bytes 16777216 | tf_op jit(solution)/shard_map/pallas_call | solution.py:436
  95.0 2.0 %copy.6 = f32[1024,1024]{1,0:T(8,128)} copy(f32[1024,1024]{1,0:T(8,128)S(1)} %shard_map.46) | data formatting | bytes 8388608

commit v4 on v3

--- a/solution.py
+++ b/solution.py
@@ -9,8 +9,8 @@
 
 MESH = pl.DeviceIdType.MESH
 F32, BF16 = jnp.float32, jnp.bfloat16
-GROUPS = ((0, 256), (256, 128), (384, 128))
-MESSAGES = 160
+GROUPS = ((0, 128), (128, 128), (256, 128), (384, 128))
+MESSAGES = 176
 NN = (((1,), (0,)), ((), ()))
 NT = (((1,), (1,)), ((), ()))
 
@@ -111,7 +111,7 @@
         copy_z[-1].start()
 
     barrier = pltpu.get_barrier_semaphore()
-    greeted = near_z + near_xy
+    greeted = [first[1], first[3], second[1], second[3], z_hi_partner, z_lo_partner, partner]
     for other_device in greeted:
         pl.semaphore_signal(barrier, inc=1, device_id=other_device, device_id_type=MESH)
     pl.semaphore_wait(barrier, len(greeted))
@@ -251,16 +251,15 @@
         ah, al = rank_rows(yy)
         u[yy] = dot3(ah, al, resh[...], resl[...], NT)
 
+    def take(j):
+        rows = slice(256 * j, 256 * j + 256)
+        u_sent[j].wait_recv()
+        uh[rows, :], ul[rows, :] = split(u[2 * core + j] + u_in[j])
+
     u_sent = []
     for j in range(2):
         project(2 * other + j)
         u_sent.append(send(u.at[2 * other + j], u_in.at[j], partner))
-    for j in range(2):
-        project(2 * core + j)
-    for j in range(2):
-        u_sent[j].wait_recv()
-        uh[256 * j : 256 * j + 256, :], ul[256 * j : 256 * j + 256, :] = split(u[2 * core + j] + u_in[j])
-
     def gradient(n0, w, a, b, e, relay, ra, acc, rb, ring):
         half = w // 2
         ia, ib, ie = (x * v[0] + y * v[1] + z * v[2] for v in (a, b, e))
@@ -342,6 +341,7 @@
     xs, ys, zs = (1, 0, 0), (0, 1, 0), (0, 0, 1)
     orders = (
         ((other, core, 0), (0, other, core), (core, 0, other)),
+        ((other, core, 0), (0, other, core), (core, 0, other)),
         ((core, other, 0), (0, core, other), (other, 0, core)),
         (zs, xs, ys),
     )
@@ -349,6 +349,16 @@
         gradient(*group, *order, *(held[i] for held in (relay, ra, acc, rb, ring)))
         for i, (group, order) in enumerate(zip(GROUPS, orders))
     ]
+    project(2 * core)
+    take(0)
+    for steps in groups[:2]:
+        next(steps)
+    project(2 * core + 1)
+    for steps in groups[:2]:
+        next(steps)
+    take(1)
+    for steps in groups[2:] * 2:
+        next(steps)
     lockstep(groups)
     inner_sent = [send(inner.at[0, i], inner.at[1, i], partner) for i in range(2)]
     g_half = g.at[:, pl.ds(aligned(512 * core, 512), 512)]

time: 97.3 us -> 91.7 us (0.942)
  Pallas kernels: 95 us -> 89.5 us
    pallas_call x1, Pallas kernels: 95 us -> 89.5 us  [shards(): pl.pallas_call(kernel, out_shape=pltpu.VMEM((1024, 1024), F32), in_specs=...]
where the time goes in v4:
time: 91.7 us; the launch traced here: 91.5 us
  Pallas kernels  89.5 us (98%)
  local copies, waits for them, and re-layouts  2.02 us (2%)
    pallas_call x1, Pallas kernels, shards(): pl.pallas_call(kernel, out_shape=pltpu.VMEM((1024, 1024), F32), in_specs=...  89.5 us
    unnamed x1, local copies, waits for them, and re-layouts  2.02 us

profile of v4, /device:TPU:0, one launch (start us, length us, event | category | flops | bytes accessed | tf_op | source)
XLA Modules:
  0.0 91.5 jit_solution(9752625548273384810)
XLA Ops:
  0.0 89.5 %shard_map.46 = f32[1024,1024]{1,0:T(8,128)S(1)} custom-call(f32[1024,512]{1,0:T(8,128)} %v_hbm.1, f32[32,1024]{1,0:T(8,128)} %bitcast.1, f32[1024,1024]{1,0:T(8,128)} %z_hbm.1, f32[512,256]{1,0:T(8,128)} %r_hbm.1), custom_call_target="tpu_custom_call" | custom-call | flops 7000000000 | bytes 16777216 | tf_op jit(solution)/shard_map/pallas_call | solution.py:446
  89.5 2.0 %copy.6 = f32[1024,1024]{1,0:T(8,128)} copy(f32[1024,1024]{1,0:T(8,128)S(1)} %shard_map.46) | data formatting | bytes 8388608

commit v5 on v4

--- a/solution.py
+++ b/solution.py
@@ -69,7 +69,7 @@
 def kernel(
     v_hbm, l_hbm, z_hbm, r_hbm, out,
     v_in, z_in, lt, r4, rest, u, u_in, g,
-    zh, zl, rh, rl, lth, ltl, mh, ml, resh, resl, uh, ul, inner, ih, il,
+    zh, zl, rh, rl, lth, ltl, mixed, mh, ml, resh, resl, uh, ul, inner, ih, il,
     gp, relay, ra, acc, rb, ring, slots_z, slots_xy, send_sems, recv_sems, local_sems,
 ):
     r, c = lax.axis_index("rows"), lax.axis_index("cols")
@@ -90,6 +90,10 @@
     second = [device(d * core, d * other, 0, core) for d in range(4)]
     i1, i2 = x * other + y * core, y * other + x * core
 
+    barrier = pltpu.get_barrier_semaphore()
+    greeted = [*first[1:], second[1], second[3], z_hi_partner, z_lo_partner, partner]
+    for other_device in greeted:
+        pl.semaphore_signal(barrier, inc=1, device_id=other_device, device_id_type=MESH)
     at_l = (i2, pl.ds(aligned(64 * i1 + 32 * z_hi, 32), 32))
     copy_l = pltpu.make_async_copy(l_hbm, lt.at[at_l], local_sems.at[0])
     copy_r = pltpu.make_async_copy(r_hbm, r4.at[r], local_sems.at[1])
@@ -110,10 +114,12 @@
         )
         copy_z[-1].start()
 
-    barrier = pltpu.get_barrier_semaphore()
-    greeted = [first[1], first[3], second[1], second[3], z_hi_partner, z_lo_partner, partner]
-    for other_device in greeted:
-        pl.semaphore_signal(barrier, inc=1, device_id=other_device, device_id_type=MESH)
+    def transpose_v(i):
+        rest[:, 128 * i : 128 * i + 128] = jnp.transpose(v_in[128 * i : 128 * i + 128, :])
+
+    copy_v.wait()
+    for i in range(8):
+        transpose_v(i)
     pl.semaphore_wait(barrier, len(greeted))
 
     send = Sender(send_sems, recv_sems)
@@ -130,35 +136,32 @@
     mine = shard(0, 0, own)
     to_z = send(mine, mine, z_hi_partner)
     near_own = spread(mine, first)
+    through_own = send(mine, mine, first[2])
     wide = {(0, "own"): spread(mine, second)}
 
     copy_r.wait()
     r_to_core = send(r4.at[r], r4.at[r], partner)
+
+    def split_z(i, _):
+        zh[i], zl[i] = split(z_in[i])
+        return 0
+
+    for copy in copy_z:
+        copy.wait()
+    lax.fori_loop(0, 4, split_z, 0)
+    to_z.wait_recv()
     r_to_z = send(r4.at[r], r4.at[r], z_lo_partner)
-
-    def transpose_v(i):
-        rest[:, 128 * i : 128 * i + 128] = jnp.transpose(v_in[128 * i : 128 * i + 128, :])
-
-    copy_v.wait()
-    for i in range(4):
-        transpose_v(i)
-
-    to_z.wait_recv()
     theirs = shard(0, 0, far)
     near_far = spread(theirs, first)
+    through_far = send(theirs, theirs, first[2])
     wide[0, "far"] = spread(theirs, second)
-    for i in range(4, 8):
-        transpose_v(i)
-
     near_own[0].wait_recv()
     ref = shard(3, 0, own)
-    through_own = send(ref, ref, first[1])
     wide[3, "own"] = spread(ref, second)
     near_own[1].wait_recv()
     wide[1, "own"] = spread(shard(1, 0, own), second)
     near_far[1].wait_recv()
     ref = shard(1, 0, far)
-    through_far = send(ref, ref, first[3])
     wide[1, "far"] = spread(ref, second)
     near_far[0].wait_recv()
     wide[3, "far"] = spread(shard(3, 0, far), second)
@@ -173,44 +176,47 @@
         ref = shard(d1, 1, far)
         passed.append(send(ref, ref, second[3]))
 
-    pass_on(0)
+    def split_r(k):
+        rh[k], rl[k] = split(r4[k])
+
+    def mix(i, chip):
+        k = pl.ds(aligned(512 * chip, 512), 512)
+        for m in (0, 256):
+            rows = slice(m, m + 256)
+            ah, al = (jnp.concatenate([ref[2 * chip + j, rows, :] for j in (0, 1)], 1) for ref in (rh, rl))
+            yield rows, dot3(ah, al, zh[i, :, k], zl[i, :, k], NT)
+
+    def mix_first(i):
+        for rows, part in mix(i, z_lo):
+            mixed[i, rows, :] = part
+
+    def mix_rest(i):
+        for rows, part in mix(i, 1 - z_lo):
+            mh[i, rows, :], ml[i, rows, :] = split(mixed[i, rows, :] + part)
+
     through_own.wait_recv()
     wide[2, "own"] = spread(shard(2, 0, own), second)
+    pass_on(0)
     through_far.wait_recv()
     wide[2, "far"] = spread(shard(2, 0, far), second)
 
-    for copy in copy_z:
-        copy.wait()
-
-    def split_z(i, _):
-        zh[i], zl[i] = split(z_in[i])
-        return 0
-
-    lax.fori_loop(0, 4, split_z, 0)
+    split_r(r)
+    r_to_core.wait_recv()
+    split_r(2 * z_lo + other)
+    mix_first(0)
     pass_on(3)
+    mix_first(1)
     pass_on(1)
+    mix_first(2)
+    mix_first(3)
 
     r_to_z.wait_recv()
     r_far = r4.at[2 * (1 - z_lo) + core]
     r_on = send(r_far, r_far, partner)
-    r_to_core.wait_recv()
+    split_r(2 * (1 - z_lo) + core)
+    pass_on(2)
     r_on.wait_recv()
-
-    def split_r(i, _):
-        rh[i], rl[i] = split(r4[i])
-        return 0
-
-    lax.fori_loop(0, 4, split_r, 0)
-
-    def mix(i, _):
-        for m in (0, 256):
-            rows = slice(m, m + 256)
-            ah, al = (jnp.concatenate([ref[k, rows, :] for k in range(4)], 1) for ref in (rh, rl))
-            mh[i, rows, :], ml[i, rows, :] = split(dot3(ah, al, zh[i], zl[i], NT))
-        return 0
-
-    mix(i2, 0)
-    mix(lax.rem(i2 + 3, 4), 0)
+    split_r(2 * (1 - z_lo) + other)
 
     def subtract(i):
         lth[i], ltl[i] = split(lt[i])
@@ -218,16 +224,17 @@
             cols = slice(n, n + 256)
             rest[:, cols] -= dot3(mh[i], ml[i], lth[i, :, cols], ltl[i, :, cols], NN)
 
-    pass_on(2)
-    mix(lax.rem(i2 + 1, 4), 0)
-    mix(lax.rem(i2 + 2, 4), 0)
+    mix_rest(i2)
     subtract(i2)
+    mix_rest(lax.rem(i2 + 3, 4))
     for d1 in range(4):
         wide[d1, "far"][0].wait_recv()
     subtract(lax.rem(i2 + 3, 4))
+    mix_rest(lax.rem(i2 + 1, 4))
     for d1 in range(4):
         wide[d1, "own"][1].wait_recv()
     subtract(lax.rem(i2 + 1, 4))
+    mix_rest(lax.rem(i2 + 2, 4))
     for copy in passed:
         copy.wait_recv()
     subtract(lax.rem(i2 + 2, 4))
@@ -430,7 +437,8 @@
         v((1024, 512), F32), v((4, 256, 1024), F32), v((4, 256, 1024), F32),
         v((4, 512, 256), F32), v((512, 1024), F32), v((4, 256, 512), F32), v((2, 256, 512), F32), v((4, 1024, 256), F32),
         v((4, 256, 1024), BF16), v((4, 256, 1024), BF16), v((4, 512, 256), BF16), v((4, 512, 256), BF16),
-        v((4, 256, 1024), BF16), v((4, 256, 1024), BF16), v((4, 512, 256), BF16), v((4, 512, 256), BF16),
+        v((4, 256, 1024), BF16), v((4, 256, 1024), BF16),
+        v((4, 512, 256), F32), v((4, 512, 256), BF16), v((4, 512, 256), BF16),
         v((512, 1024), BF16), v((512, 1024), BF16), v((512, 512), BF16), v((512, 512), BF16),
         v((2, 2, 512, 256), F32), v((512, 256), BF16), v((512, 256), BF16),
         v((4, 512, 256), F32), [v((2, w // 2, 256), F32) for w in rows], [v((2, w, 256), F32) for w in rows],

time: 91.7 us -> 90.7 us (0.989)
  Pallas kernels: 89.5 us -> 88.4 us
    pallas_call x1, Pallas kernels: 89.5 us -> 88.4 us  [shards(): pl.pallas_call(kernel, out_shape=pltpu.VMEM((1024, 1024), F32), in_specs=...]
where the time goes in v5:
time: 90.7 us; the launch traced here: 90.5 us
  Pallas kernels  88.4 us (97%)
  local copies, waits for them, and re-layouts  2.02 us (2%)
    pallas_call x1, Pallas kernels, shards(): pl.pallas_call(kernel, out_shape=pltpu.VMEM((1024, 1024), F32), in_specs=...  88.4 us
    unnamed x1, local copies, waits for them, and re-layouts  2.02 us

profile of v5, /device:TPU:0, one launch (start us, length us, event | category | flops | bytes accessed | tf_op | source)
XLA Modules:
  0.0 90.5 jit_solution(1442630067954419607)
XLA Ops:
  0.0 88.4 %shard_map.46 = f32[1024,1024]{1,0:T(8,128)S(1)} custom-call(f32[1024,512]{1,0:T(8,128)} %v_hbm.1, f32[32,1024]{1,0:T(8,128)} %bitcast.1, f32[1024,1024]{1,0:T(8,128)} %z_hbm.1, f32[512,256]{1,0:T(8,128)} %r_hbm.1), custom_call_target="tpu_custom_call" | custom-call | flops 7000000000 | bytes 16777216 | tf_op jit(solution)/shard_map/pallas_call | solution.py:454
  88.4 2.0 %copy.6 = f32[1024,1024]{1,0:T(8,128)} copy(f32[1024,1024]{1,0:T(8,128)S(1)} %shard_map.46) | data formatting | bytes 8388608
